TPU v7x, 32 devices: a whole 2x2x4 slice. The times are simulated.
32 devices in a mesh: row: 2 (over x), col: 16 (over z, y, core).
Axes of the slice: x: 2, y: 2, z: 4, core: 2. Of those that a mesh axis runs over, the one named last changes fastest.
Arguments:
- pair: float32 [128, 128, 128], P('row', 'col'), may hold values from -6 to 6
- single: float32 [128, 384], P(('row', 'col')), may hold values from -6 to 6
- target_bins: int32 [128, 128], P('row', 'col'), may hold values from 0 to 63
- token_pad: int32 [128], P(('row', 'col')), may hold values from 0 to 1, as said below
- w_gate: float32 [128, 512], replicated, may hold values from -0.5 to 0.5
- w_up: float32 [128, 512], replicated, may hold values from -0.5 to 0.5
- w_out: float32 [512, 128], replicated, may hold values from -0.25 to 0.25
- w_bias: float32 [128, 16], replicated, may hold values from -25 to 25
- w_query: float32 [384, 384], replicated, may hold values from -0.3125 to 0.3125
- w_key: float32 [384, 384], replicated, may hold values from -0.3125 to 0.3125
- w_value: float32 [384, 384], replicated, may hold values from -0.3125 to 0.3125
- w_gating: float32 [384, 384], replicated, may hold values from -0.3125 to 0.3125
- w_attn_out: float32 [384, 384], replicated, may hold values from -0.3125 to 0.3125
- w_dist: float32 [128, 64], replicated, may hold values from -12 to 12
- b_dist: float32 [64], replicated, may hold values from -2 to 2
Outputs:
- pair_out: float32 [128, 128, 128], P('row', 'col')
- single_out: float32 [128, 384], P(('row', 'col'))
Inputs may be any that keep to these rules, and one draw needn't show every extreme that they name: `token_pad`: 1 for the first tokens and 0 for the rest, with at least 64 ones.
All inputs are finite; a program needn't handle non-finite values.
Results may differ from a plain program's by a relative error of at most 0.0003.
Values sent between devices are 32-bit elements; how exact they have to be, the bound alone decides.
A program may use at most 64 MiB of HBM per device.

v0:
```python
import jax
import jax.numpy as jnp
from jax import lax
from jax.sharding import PartitionSpec as P

HI = lax.Precision.HIGHEST


def joined(value, axis, join):
    pieces = jax.tree.map(lambda part: lax.all_gather(part, axis), value)
    head = jax.tree.map(lambda part: part[0], pieces)
    tail = jax.tree.map(lambda part: part[1:], pieces)
    total, _ = lax.scan(lambda total, piece: (join(total, piece), None), head, tail)
    return total


def layer_norm(x):
    mean = jnp.mean(x, axis=-1, keepdims=True)
    centred = x - mean
    var = jnp.mean(centred * centred, axis=-1, keepdims=True)
    return centred * lax.rsqrt(var + 1e-05)


def dense(x, w):
    flat = x.reshape(-1, x.shape[-1])
    out = jnp.dot(flat, w, precision=HI, preferred_element_type=jnp.float32)
    return out.reshape(x.shape[:-1] + (w.shape[1],))


def softmax_bins(logits):
    shifted = logits - jnp.max(logits, axis=-1, keepdims=True)
    expo = jnp.exp(shifted)
    return expo / jnp.sum(expo, axis=-1, keepdims=True)


def per_device(
    pair,
    single,
    target_bins,
    token_pad,
    w_gate,
    w_up,
    w_out,
    w_bias,
    w_query,
    w_key,
    w_value,
    w_gating,
    w_attn_out,
    w_dist,
    b_dist,
):
    rows, cols, width = pair.shape
    n_row = lax.axis_size("row")
    n_col = lax.axis_size("col")
    tok_dev, single_width = single.shape
    heads = w_bias.shape[1]
    bins = w_dist.shape[1]
    head_dim = single_width // heads
    quarter = rows // 4

    def block_step(piece):
        normed = layer_norm(piece)
        hidden = jax.nn.silu(dense(normed, w_gate)) * dense(normed, w_up)
        mid_piece = piece + dense(hidden, w_out)
        return (mid_piece, dense(layer_norm(mid_piece), w_bias), dense(mid_piece, w_dist))

    mid, bias, proj = lax.map(block_step, pair.reshape(4, quarter, cols, width))
    mid = mid.reshape(rows, cols, width)
    bias = bias.reshape(rows, cols, heads)
    proj = proj.reshape(rows, cols * bins)
    single_norm = layer_norm(single)
    query = dense(single_norm, w_query)
    key = dense(single_norm, w_key)
    value = dense(single_norm, w_value)
    gating = jax.nn.sigmoid(dense(single_norm, w_gating))
    pad_float = token_pad.astype(jnp.float32)
    queries, key_rows, value_rows, pad_rows = (
        lax.all_gather(query, "col", axis=0, tiled=True),
        lax.all_gather(key, "col", axis=0, tiled=True),
        lax.all_gather(value, "col", axis=0, tiled=True),
        lax.all_gather(pad_float, "col", axis=0, tiled=True),
    )
    keys_all, values_all, pad_all = (
        lax.all_gather(key_rows, "row", axis=0, tiled=True),
        lax.all_gather(value_rows, "row", axis=0, tiled=True),
        lax.all_gather(pad_rows, "row", axis=0, tiled=True),
    )
    col_index = lax.axis_index("col")
    start = col_index * cols
    key_block = lax.dynamic_slice_in_dim(keys_all, start, cols, 0).reshape(cols, heads, head_dim)
    value_block = lax.dynamic_slice_in_dim(values_all, start, cols, 0).reshape(
        cols, heads, head_dim
    )
    pad_block = lax.dynamic_slice_in_dim(pad_all, start, cols, 0)
    scale = 1.0 / jnp.sqrt(jnp.float32(head_dim))
    scores = (
        jnp.einsum("ihd,jhd->ijh", queries.reshape(rows, heads, head_dim), key_block, precision=HI)
        * scale
        + bias
    )
    scores = jnp.where(pad_block[None, :, None] > 0.5, scores, jnp.float32(-1000000000.0))
    local_max = jnp.max(scores, axis=1)
    expo = jnp.exp(scores - local_max[:, None, :])
    local_sum = jnp.sum(expo, axis=1)
    local_acc = jnp.einsum("ijh,jhd->ihd", expo, value_block, precision=HI)
    mine = col_index * tok_dev

    def combine(first, second):
        top_a, sum_a, acc_a = first
        top_b, sum_b, acc_b = second
        top = jnp.maximum(top_a, top_b)
        factor_a = jnp.exp(top_a - top)
        factor_b = jnp.exp(top_b - top)
        count = acc_a.shape[0]
        acc = (
            acc_a.reshape(count, heads, head_dim) * factor_a[:, :, None]
            + acc_b.reshape(count, heads, head_dim) * factor_b[:, :, None]
        )
        return (top, sum_a * factor_a + sum_b * factor_b, acc.reshape(count, heads * head_dim))

    top, total, acc = joined(
        (local_max, local_sum, local_acc.reshape(rows, single_width)), "col", combine
    )
    total = lax.dynamic_slice_in_dim(total, mine, tok_dev, 0)
    acc = lax.dynamic_slice_in_dim(acc, mine, tok_dev, 0)
    attended = (acc.reshape(tok_dev, heads, head_dim) / total[:, :, None]).reshape(
        tok_dev, single_width
    )
    single_out = single + dense(gating * attended, w_attn_out)
    proj_rows, target_rows = (
        lax.all_to_all(proj, "col", split_axis=0, concat_axis=1, tiled=True),
        lax.all_to_all(
            target_bins.astype(jnp.float32), "col", split_axis=0, concat_axis=1, tiled=True
        ),
    )
    total_tokens = target_rows.shape[1]

    def to_blocks(x, inner):
        return x.reshape(tok_dev, n_row, n_col, tok_dev * inner)

    def from_blocks(y, inner):
        parts = y.reshape(tok_dev, n_row, n_col, tok_dev, inner)
        return jnp.transpose(parts, (3, 1, 2, 0, 4)).reshape(tok_dev, total_tokens, inner)

    proj_flat = proj_rows.reshape(tok_dev, total_tokens, bins)
    mask = pad_float[:, None] * pad_all[None, :]
    bin_ids = jnp.arange(bins, dtype=jnp.float32)
    onehot = (target_rows[:, :, None] == bin_ids).astype(jnp.float32)
    flipped = lax.all_to_all(
        lax.all_to_all(to_blocks(proj_rows, bins), "row", split_axis=1, concat_axis=1, tiled=True),
        "col",
        split_axis=2,
        concat_axis=2,
        tiled=True,
    )
    probs = softmax_bins(proj_flat + from_blocks(flipped, bins) + b_dist)
    grad = mask[:, :, None] * (probs - onehot)
    grad_flip = lax.all_to_all(
        lax.all_to_all(to_blocks(grad, bins), "row", split_axis=1, concat_axis=1, tiled=True),
        "col",
        split_axis=2,
        concat_axis=2,
        tiled=True,
    )
    delta = grad + from_blocks(grad_flip, bins)
    delta_tiles = lax.all_to_all(
        delta.reshape(tok_dev, total_tokens * bins), "col", split_axis=1, concat_axis=0, tiled=True
    )
    change = dense(delta_tiles.reshape(rows, cols, bins), jnp.transpose(w_dist))
    pair_out = mid + change
    return (pair_out, single_out)


def solution(mesh):
    in_specs = (
        P("row", "col", None),
        P(("row", "col"), None),
        P("row", "col"),
        P(("row", "col")),
        P(),
        P(),
        P(),
        P(),
        P(),
        P(),
        P(),
        P(),
        P(),
        P(),
        P(),
    )
    out_specs = (P("row", "col", None), P(("row", "col"), None))
    return jax.shard_map(
        per_device, mesh=mesh, in_specs=in_specs, out_specs=out_specs, check_vma=False
    )
```

profile of v0, /device:TPU:0, one launch (start us, length us, event | category | flops | bytes accessed | tf_op | source)
XLA Modules:
  0.0 258.8 jit_solution(6004236540770849275)
XLA Ops:
  7.3 1.3 dynamic-slice.1
  8.6 1.3 dynamic-slice
  9.9 0.8 reduce_sum.73
  10.7 0.9 multiply_reduce_fusion.2
  12.3 0.8 convert_dynamic-update-slice_fusion
  13.0 34.9 %all-reduce = f32[64]{0:T(128)S(1)} all-reduce(f32[64]{0:T(128)S(1)} %convert_dynamic-update-slice_fusion), channel_id=1, replica_groups=mesh['row'=2,'col'=16] {'col'}, use_global_device_ids=true, to_apply=%add | all-reduce | flops 64 | bytes 512
  48.6 0.2 dynamic-update-slice.1
  48.8 4.9 %all-reduce.1 = f32[128]{0:T(128)S(1)} all-reduce(f32[128]{0:T(128)S(1)} %dynamic-update-slice.1), channel_id=1, replica_groups=mesh['row'=2,'col'=16] {'row'}, use_global_device_ids=true, to_apply=%add.1 | all-reduce | flops 128 | bytes 1024
  53.8 1.2 convolution_bitcast_fusion.4
  55.0 1.5 convolution_bitcast_fusion.3
  56.5 1.5 convolution_bitcast_fusion.2
  58.0 17.4 %all-gather.6 = f32[16,4,384]{2,1,0:T(4,128)S(1)} all-gather(f32[1,4,384]{2,1,0:T(4,128)S(1)} %convolution_bitcast_fusion.2), channel_id=1, replica_groups=mesh['row'=2,'col'=16] {'col'}, dimensions={0}, use_global_device_ids=true | all-gather | bytes 104448 | tf_op jit(solution)/shard_map/all_gather | solution.py:81
  75.4 19.3 %all-gather.3 = f32[16,4,384]{2,1,0:T(4,128)S(1)} all-gather(f32[1,4,384]{2,1,0:T(4,128)S(1)} %convolution_bitcast_fusion.3), channel_id=1, replica_groups=mesh['row'=2,'col'=16] {'col'}, dimensions={0}, use_global_device_ids=true | all-gather | bytes 104448 | tf_op jit(solution)/shard_map/all_gather | solution.py:79
  94.8 17.7 %all-gather.2 = f32[16,4,384]{2,1,0:T(4,128)S(1)} all-gather(f32[1,4,384]{2,1,0:T(4,128)S(1)} %convolution_bitcast_fusion.4), channel_id=1, replica_groups=mesh['row'=2,'col'=16] {'col'}, dimensions={0}, use_global_device_ids=true | all-gather | bytes 104448 | tf_op jit(solution)/shard_map/all_gather | solution.py:80
  112.5 5.7 %all_gather.39 = f32[128,384]{1,0:T(8,128)S(1)} all-gather(f32[64,384]{1,0:T(8,128)S(1)} %reshape.267), channel_id=1, replica_groups=mesh['row'=2,'col'=16] {'row'}, dimensions={0}, use_global_device_ids=true | all-gather | bytes 294912 | tf_op jit(solution)/shard_map/all_gather | solution.py:85
  118.4 5.3 %all_gather.46 = f32[128,384]{1,0:T(8,128)S(1)} all-gather(f32[64,384]{1,0:T(8,128)S(1)} %reshape.275), channel_id=1, replica_groups=mesh['row'=2,'col'=16] {'row'}, dimensions={0}, use_global_device_ids=true | all-gather | bytes 294912 | tf_op jit(solution)/shard_map/all_gather | solution.py:86
  123.8 9.3 %while.28 = (s32[]{:T(128)}, f32[4,16,8,128]{3,2,1,0:T(8,128)S(1)}, f32[4,16,8,16]{3,2,1,0:T(8,128)S(1)}, f32[4,16,8,64]{3,2,1,0:T(8,128)S(1)}, f32[4,16,8,128]{...) while((s32[]{:T(128)}, f32[4,16,8,128]{3,2,1,0:T(8,128)S(1)}, ...), condition=%wide.region_5.6_spmd, body=%wide.region_0.5_spmd.sunk | while | flops 318292224 | bytes 2784413 | solution.py:68
  124.1 0.4 fusion.75
  124.6 0.4 convolution_multiply_fusion.3
  125.0 0.4 bitcast_dynamic-update-slice_fusion.2
  125.7 0.3 fusion.76
  126.5 0.4 fusion.75
  126.9 0.4 convolution_multiply_fusion.3
  127.3 0.4 bitcast_dynamic-update-slice_fusion.2
  128.0 0.3 fusion.76
  128.8 0.4 fusion.75
  129.2 0.4 convolution_multiply_fusion.3
  129.7 0.4 bitcast_dynamic-update-slice_fusion.2
  130.4 0.3 fusion.76
  131.1 0.4 fusion.75
  131.6 0.4 convolution_multiply_fusion.3
  132.0 0.4 bitcast_dynamic-update-slice_fusion.2
  132.7 0.3 fusion.76
  133.3 0.4 reshape.249
  133.7 1.1 fusion.42
  134.8 0.6 fusion.35
  135.3 0.8 copy.59
  136.2 10.8 %all_to_all.65 = f32[16,4,512]{2,1,0:T(4,128)S(1)} all-to-all(f32[16,4,512]{2,1,0:T(4,128)S(1)} %all_to_all.46), channel_id=1, replica_groups=mesh['row'=2,'col'=16] {'col'}, dimensions={0} | all-to-all | bytes 262144 | tf_op jit(solution)/shard_map/all_to_all | solution.py:132
  147.1 0.7 copy.46
  147.8 3.4 %all-to-all-start.1 = ((f32[4,2,16,256]{3,2,0,1:T(8,128)}), f32[4,2,16,256]{3,2,0,1:T(8,128)S(1)}, u32[]{:S(2)}, u32[]{:S(2)}) async-start(f32[4,2,16,256]{3,2,0,1:T(8,128)} %copy.46), calls=%async_computation.1 | async-start | bytes 262144 | tf_op jit(solution)/shard_map/all_to_all | solution.py:151
  151.2 0.7 copy.49
  151.9 3.8 %all-to-all-done.1 = f32[4,2,16,256]{3,2,0,1:T(8,128)S(1)} async-done(((f32[4,2,16,256]{3,2,0,1:T(8,128)}), f32[4,2,16,256]{3,2,0,1:T(8,128)S(1)}, u32[]{:S(2)}, u32[]{:S(2)}) %all-to-all-start.1) | async-done | bytes 131104 | tf_op jit(solution)/shard_map/all_to_all | solution.py:151
  155.6 3.5 %all-to-all-start.3 = ((f32[16,4,8]{2,1,0:T(4,128)}), f32[16,4,8]{2,1,0:T(4,128)S(1)}, u32[]{:S(2)}, u32[]{:S(2)}) async-start(f32[16,4,8]{2,1,0:T(4,128)} %bitcast.21), calls=%async_computation.3 | async-start | bytes 65536 | tf_op jit(solution)/shard_map/all_to_all | solution.py:133
  159.1 0.8 copy.47
  159.9 6.3 %all-to-all-done.3 = f32[16,4,8]{2,1,0:T(4,128)S(1)} async-done(((f32[16,4,8]{2,1,0:T(4,128)}), f32[16,4,8]{2,1,0:T(4,128)S(1)}, u32[]{:S(2)}, u32[]{:S(2)}) %all-to-all-start.3) | async-done | bytes 2080 | tf_op jit(solution)/shard_map/all_to_all | solution.py:133
  166.1 3.5 %all-to-all-start.2 = ((f32[4,2,16,256]{3,1,0,2:T(2,128)}), f32[4,2,16,256]{3,1,0,2:T(2,128)S(1)}, u32[]{:S(2)}, u32[]{:S(2)}) async-start(f32[4,2,16,256]{3,1,0,2:T(2,128)} %copy.47), calls=%async_computation.2 | async-start | bytes 262144 | tf_op jit(solution)/shard_map/all_to_all | solution.py:150
  170.9 6.6 %all-to-all-done.2 = f32[4,2,16,256]{3,1,0,2:T(2,128)S(1)} async-done(((f32[4,2,16,256]{3,1,0,2:T(2,128)}), f32[4,2,16,256]{3,1,0,2:T(2,128)S(1)}, u32[]{:S(2)}, u32[]{:S(2)}) %all-to-all-start.2) | async-done | bytes 131104 | tf_op jit(solution)/shard_map/all_to_all | solution.py:150
  178.5 0.3 exponential_reduce_fusion
  179.1 0.7 copy.51
  179.7 3.4 %all-to-all-start.4 = ((f32[4,2,16,256]{3,2,0,1:T(8,128)}), f32[4,2,16,256]{3,2,0,1:T(8,128)S(1)}, u32[]{:S(2)}, u32[]{:S(2)}) async-start(f32[4,2,16,256]{3,2,0,1:T(8,128)} %copy.51), calls=%async_computation.4 | async-start | bytes 262144 | tf_op jit(solution)/shard_map/all_to_all | solution.py:160
  183.2 4.4 %all-to-all-done.4 = f32[4,2,16,256]{3,2,0,1:T(8,128)S(1)} async-done(((f32[4,2,16,256]{3,2,0,1:T(8,128)}), f32[4,2,16,256]{3,2,0,1:T(8,128)S(1)}, u32[]{:S(2)}, u32[]{:S(2)}) %all-to-all-start.4) | async-done | bytes 131104 | tf_op jit(solution)/shard_map/all_to_all | solution.py:160
  187.6 0.8 copy.52
  188.3 3.5 %all-to-all-start.5 = ((f32[4,2,16,256]{3,1,0,2:T(2,128)}), f32[4,2,16,256]{3,1,0,2:T(2,128)S(1)}, u32[]{:S(2)}, u32[]{:S(2)}) async-start(f32[4,2,16,256]{3,1,0,2:T(2,128)} %copy.52), calls=%async_computation.5 | async-start | bytes 262144 | tf_op jit(solution)/shard_map/all_to_all | solution.py:159
  191.9 22.0 %all-gather.5 = f32[16,64,16]{1,2,0:T(8,128)S(1)} all-gather(f32[1,64,16]{1,2,0:T(8,128)S(1)} %bitcast.167), channel_id=3, replica_groups=mesh['row'=2,'col'=16] {'col'}, dimensions={0}, use_global_device_ids=true | all-gather | bytes 69632 | tf_op jit(solution)/shard_map/all_gather | solution.py:10
  214.4 0.2 reshape.246
  215.0 0.7 copy.54
  215.7 3.5 %all-to-all-start.6 = ((f32[4,16,512]{2,0,1:T(4,128)}), f32[4,16,512]{2,0,1:T(4,128)S(1)}, u32[]{:S(2)}, u32[]{:S(2)}) async-start(f32[4,16,512]{2,0,1:T(4,128)} %copy.54), calls=%async_computation.6 | async-start | bytes 262144 | tf_op jit(solution)/shard_map/all_to_all | solution.py:167
  219.2 22.0 %all-gather.4 = f32[16,64,16]{1,2,0:T(8,128)S(1)} all-gather(f32[1,64,16]{1,2,0:T(8,128)S(1)} %bitcast.165), channel_id=2, replica_groups=mesh['row'=2,'col'=16] {'col'}, dimensions={0}, use_global_device_ids=true | all-gather | bytes 69632 | tf_op jit(solution)/shard_map/all_gather | solution.py:10
  241.4 1.1 convolution_add_fusion.1
  242.5 0.9 slice_bitcast_fusion
  243.5 1.2 slice-done
  244.8 4.2 %while.29 = (s32[]{:T(128)}, f32[64,16]{0,1:T(8,128)S(1)}, f32[64,16]{0,1:T(8,128)S(1)}, f32[64,384]{0,1:T(8,128)S(1)}, f32[15,64,16]{1,2,0:T(8,128)S(1)}, /*ind...) while((s32[]{:T(128)}, f32[64,16]{0,1:T(8,128)S(1)}, f32[64,16]{0,1:T(8,128)S(1)}, ...), condition=%wide.region_13.14_spmd, body=%wide.region_12.13_spmd.sunk | while | flops 79874 | bytes 729189 | solution.py:13
  249.4 0.4 fusion.32
  249.9 2.1 convolution_add_fusion.2
  (194 shorter events, 11.3 us)
Async XLA Ops:
  7.2 46.6 %copy-start = (f32[384,384]{1,0:T(8,128)S(1)}, f32[384,384]{1,0:T(8,128)}, u32[]{:S(2)}) copy-start(f32[384,384]{1,0:T(8,128)} %param.28) | copy-start | bytes 1769476
  7.2 235.3 %all-gather.9.cloned.1.call-start = ((), (), s32[]{:S(2)}) async-start(), calls=%async_computation.7 | async-start | bytes 1671168 | tf_op jit(solution)/shard_map/all_gather | solution.py:10
  53.7 70.1 %copy-start.1 = (f32[128,512]{1,0:T(8,128)S(1)}, f32[128,512]{1,0:T(8,128)}, u32[]{:S(2)}) copy-start(f32[128,512]{1,0:T(8,128)} %param.23) | copy-start | bytes 786436
  53.7 70.1 %copy-start.2 = (f32[512,128]{1,0:T(8,128)S(1)}, f32[512,128]{1,0:T(8,128)}, u32[]{:S(2)}) copy-start(f32[512,128]{1,0:T(8,128)} %param.25) | copy-start | bytes 786436
  53.7 70.1 %copy-start.3 = (f32[64,8,128]{2,1,0:T(8,128)S(1)}, f32[64,8,128]{2,1,0:T(8,128)}, u32[]{:S(2)}) copy-start(f32[64,8,128]{2,1,0:T(8,128)} %param.19) | copy-start | bytes 786436
  53.7 70.1 %copy-start.4 = (f32[128,64]{0,1:T(8,128)S(1)}, f32[128,64]{0,1:T(8,128)}, u32[]{:S(2)}) copy-start(f32[128,64]{0,1:T(8,128)} %param.32) | copy-start | bytes 98308
  53.7 70.1 %copy-start.10 = (f32[128,512]{1,0:T(8,128)S(1)}, f32[128,512]{1,0:T(8,128)}, u32[]{:S(2)}) copy-start(f32[128,512]{1,0:T(8,128)} %param.24) | copy-start | bytes 786436
  53.8 70.1 %copy-start.11 = (f32[128,16]{0,1:T(8,128)S(1)}, f32[128,16]{0,1:T(8,128)}, u32[]{:S(2)}) copy-start(f32[128,16]{0,1:T(8,128)} %param.26) | copy-start | bytes 24580
  133.7 17.5 %copy-start.9 = (s32[64,8]{0,1:T(8,128)S(1)}, s32[64,8]{0,1:T(8,128)}, u32[]{:S(2)}) copy-start(s32[64,8]{0,1:T(8,128)} %param.21) | copy-start | bytes 6148
  134.8 34.9 %copy-start.12 = (s32[4]{0:T(128)S(1)}, s32[4]{0:T(128)}, u32[]{:S(2)}) copy-start(s32[4]{0:T(128)} %param.22) | copy-start | bytes 52
  136.2 33.9 %copy-start.8 = (f32[64]{0:T(128)S(1)}, f32[64]{0:T(128)}, u32[]{:S(2)}) copy-start(f32[64]{0:T(128)} %param.33) | copy-start | bytes 772
  147.8 7.8 %all-to-all-start.1 = ((f32[4,2,16,256]{3,2,0,1:T(8,128)}), f32[4,2,16,256]{3,2,0,1:T(8,128)S(1)}, u32[]{:S(2)}, u32[]{:S(2)}) async-start(f32[4,2,16,256]{3,2,0,1:T(8,128)} %copy.46), calls=%async_computation.1 | async-start | bytes 262144 | tf_op jit(solution)/shard_map/all_to_all | solution.py:151
  155.6 10.5 %all-to-all-start.3 = ((f32[16,4,8]{2,1,0:T(4,128)}), f32[16,4,8]{2,1,0:T(4,128)S(1)}, u32[]{:S(2)}, u32[]{:S(2)}) async-start(f32[16,4,8]{2,1,0:T(4,128)} %bitcast.21), calls=%async_computation.3 | async-start | bytes 65536 | tf_op jit(solution)/shard_map/all_to_all | solution.py:133
  166.1 11.4 %all-to-all-start.2 = ((f32[4,2,16,256]{3,1,0,2:T(2,128)}), f32[4,2,16,256]{3,1,0,2:T(2,128)S(1)}, u32[]{:S(2)}, u32[]{:S(2)}) async-start(f32[4,2,16,256]{3,1,0,2:T(2,128)} %copy.47), calls=%async_computation.2 | async-start | bytes 262144 | tf_op jit(solution)/shard_map/all_to_all | solution.py:150
  179.7 7.8 %all-to-all-start.4 = ((f32[4,2,16,256]{3,2,0,1:T(8,128)}), f32[4,2,16,256]{3,2,0,1:T(8,128)S(1)}, u32[]{:S(2)}, u32[]{:S(2)}) async-start(f32[4,2,16,256]{3,2,0,1:T(8,128)} %copy.51), calls=%async_computation.4 | async-start | bytes 262144 | tf_op jit(solution)/shard_map/all_to_all | solution.py:160
  188.3 26.1 %all-to-all-start.5 = ((f32[4,2,16,256]{3,1,0,2:T(2,128)}), f32[4,2,16,256]{3,1,0,2:T(2,128)S(1)}, u32[]{:S(2)}, u32[]{:S(2)}) async-start(f32[4,2,16,256]{3,1,0,2:T(2,128)} %copy.52), calls=%async_computation.5 | async-start | bytes 262144 | tf_op jit(solution)/shard_map/all_to_all | solution.py:159
  213.9 1.0 copy-start.6
  215.7 25.6 %all-to-all-start.6 = ((f32[4,16,512]{2,0,1:T(4,128)}), f32[4,16,512]{2,0,1:T(4,128)S(1)}, u32[]{:S(2)}, u32[]{:S(2)}) async-start(f32[4,16,512]{2,0,1:T(4,128)} %copy.54), calls=%async_computation.6 | async-start | bytes 262144 | tf_op jit(solution)/shard_map/all_to_all | solution.py:167
  243.4 1.4 slice-start
  243.4 1.4 slice-start.1
  244.8 4.6 %copy-start.5 = (f32[384,384]{1,0:T(8,128)S(1)}, f32[384,384]{1,0:T(8,128)}, u32[]{:S(2)}) copy-start(f32[384,384]{1,0:T(8,128)} %param.30) | copy-start | bytes 1769476
  244.8 4.7 %copy-start.7 = (f32[4,384]{1,0:T(4,128)S(1)}, f32[4,384]{1,0:T(4,128)}, u32[]{:S(2)}) copy-start(f32[4,384]{1,0:T(4,128)} %param.20) | copy-start | bytes 18436
Sparse Core Ops, SparseCore 0:
  136.2 38.4 all-gather.8
where the time goes:
time: 260 us; the launch traced here: 259 us
  blocking collectives  160 us (62%)
  waiting for transfers between devices  21.1 us (8%)
  starting transfers between devices  20.8 us (8%)
  local copies, waits for them, and re-layouts  16.9 us (6%)
  matrix products  16.2 us (6%)
  between operations  15.8 us (6%)
  other arithmetic  6.81 us (3%)
    all_gather x2, blocking collectives, joined(): pieces = jax.tree.map(lambda part: lax.all_gather(part, axis), value)  44 us
    unnamed x2, blocking collectives  39.8 us
    all_gather x1, blocking collectives, per_device(): lax.all_gather(query, 'col', axis=0, tiled=True)  19.3 us
    all_gather x1, blocking collectives, per_device(): lax.all_gather(key, 'col', axis=0, tiled=True)  17.7 us
    all_gather x1, blocking collectives, per_device(): lax.all_gather(value, 'col', axis=0, tiled=True)  17.4 us
    dot_general x26, matrix products, dense(): out = jnp.dot(flat, w, precision=HI, preferred_element_type=jnp.float32)  14.6 us
    all_to_all x1, blocking collectives, per_device(): lax.all_to_all(proj, 'col', split_axis=0, concat_axis=1, tiled=True)  10.8 us
    all_to_all x1, waiting for transfers between devices, per_device(): lax.all_to_all(lax.all_to_all(to_blocks(proj_rows, bins), 'row', split_ax...  6.61 us
  transfers between devices with their start and end apart: 7, of which 4 were waited for; matrix products, arithmetic and copies ran while one was open for 4% of the time, Pallas kernels for 0%

commit v1 on v0

v1 whole, which is shorter than its diff:
```python
import functools

import jax
import jax.numpy as jnp
from jax import lax
from jax.experimental import pallas as pl
from jax.experimental.pallas import tpu as pltpu
from jax.sharding import PartitionSpec as P

MESH = pl.DeviceIdType.MESH
F32 = jnp.float32
BF16 = jnp.bfloat16
NN = (((1,), (0,)), ((), ()))
NT = (((1,), (1,)), ((), ()))
PARTS = 2


def split(x):
    high = x.astype(BF16)
    return high, (x - high.astype(F32)).astype(BF16)


def mm(a, b, dims=NN):
    return lax.dot_general(a, b, dims, preferred_element_type=F32)


def dot3(a, b, dims=NN):
    ah, al = split(a)
    bh, bl = b if isinstance(b, tuple) else split(b)
    return mm(ah, bh, dims) + (mm(al, bh, dims) + mm(ah, bl, dims))


def layer_norm(x):
    mean = jnp.mean(x, axis=-1, keepdims=True)
    centred = x - mean
    var = jnp.mean(centred * centred, axis=-1, keepdims=True)
    return centred * lax.rsqrt(var + 1e-05)


def iota(shape, axis):
    return lax.broadcasted_iota(jnp.int32, shape, axis)


def kernel(n_row, n_col, heads, *refs):
    (pair_h, single_h, target_h, pad_s, gate_h, up_h, wout_h, wbias_h, wq_h, wk_h, wv_h, wg_h, wo_h, wdist_h, bdist_h,
     pair_o, single_o,
     pair_v, single_v, target_v, gate_v, up_v, wout_v, wbias_v, wq_v, wk_v, wv_v, wg_v, wo_v, wdist_v, bdist_v,
     ext, gath, tokens, mid_v, proj_v, flip_v, sbuf, rbuf, bsend, brecv,
     in_sem, g_send, g_recv, b_send, b_recv, p_send, p_recv) = refs
    rows, cols, width = pair_v.shape
    tok, single_width = single_v.shape
    bins = wdist_v.shape[1]
    n_dev = n_row * n_col
    group = rows // cols
    lanes = bsend.shape[2]
    head_dim = single_width // heads
    packed = cols * cols // 2
    r = lax.axis_index("row")
    c = lax.axis_index("col")
    me = r * n_col + c

    sources = (single_h, pair_h, gate_h, up_h, wout_h, target_h, wbias_h, wdist_h, wk_h, wv_h, wq_h, wg_h, wo_h, bdist_h)
    targets = (single_v, pair_v, gate_v, up_v, wout_v, target_v, wbias_v, wdist_v, wk_v, wv_v, wq_v, wg_v, wo_v, bdist_v)
    loads = [pltpu.make_async_copy(a, b, in_sem.at[k]) for k, (a, b) in enumerate(zip(sources, targets))]
    for load in loads:
        load.start()

    barrier = pltpu.get_barrier_semaphore()

    def other(step):
        d = lax.rem(me + step, n_dev)
        return d // n_col, lax.rem(d, n_col)

    def greet(step, carry):
        pl.semaphore_signal(barrier, inc=1, device_id=other(step), device_id_type=MESH)
        return carry

    lax.fori_loop(1, n_dev, greet, 0)

    loads[0].wait()
    row_id = iota((tok, 128), 0)
    pad_tile = jnp.zeros((tok, 128), F32)
    for q in range(tok):
        pad_tile = jnp.where(row_id == q, pad_s[q].astype(F32), pad_tile)
    ext[:, :single_width] = single_v[...]
    ext[:, single_width:] = pad_tile
    gath[me] = ext[...]
    pl.semaphore_wait(barrier, n_dev - 1)

    def share(step, carry):
        pltpu.make_async_remote_copy(ext, gath.at[me], g_send, g_recv, device_id=other(step), device_id_type=MESH).start()
        return carry

    lax.fori_loop(1, n_dev, share, 0)

    for load in loads[1:8]:
        load.wait()

    gate_w = split(gate_v[...])
    up_w = split(up_v[...])
    out_w = split(wout_v[...])
    wdist = wdist_v[...]
    dist_w = split(wdist)
    none = jnp.zeros_like(wdist)
    wide = jnp.concatenate([jnp.concatenate([wdist, none], axis=1), jnp.concatenate([none, wdist], axis=1)], axis=0)
    wide_w = split(wide)
    spread = (iota((heads, lanes), 0) == lax.rem(iota((heads, lanes), 1), heads)).astype(F32)
    bias_rep = lax.dot_general(wbias_v[...], spread, NN, precision=lax.Precision.HIGHEST, preferred_element_type=F32)
    lane_q = iota((width, lanes), 1) // heads
    bias_w = split(jnp.concatenate([jnp.where(lane_q == q, bias_rep, 0.0) for q in range(tok)], axis=0))

    sbuf[:, packed:, :] = jnp.zeros((group, cols, 128), F32)
    sbuf[:, packed:, :cols] = target_v[...].astype(F32).reshape(group, cols, cols)

    part = rows // PARTS
    p_row = c // group
    p_slot = lax.rem(c, group)

    def send_bias(d, carry):
        @pl.when(d != c)
        def _():
            pltpu.make_async_remote_copy(bsend.at[d], brecv.at[c], b_send, b_recv, device_id=(r, d), device_id_type=MESH).start()
        return carry

    def is_self(k):
        return jnp.logical_and(p_row == r, p_slot == k)

    def send_proj(k, carry):
        @pl.when(jnp.logical_not(is_self(k)))
        def _():
            pltpu.make_async_remote_copy(sbuf.at[k], rbuf.at[p_slot], p_send, p_recv, device_id=(p_row, group * r + k), device_id_type=MESH).start()
        return carry

    for s in range(PARTS):
        first = s * part
        x = pair_v[first:first + part].reshape(part * cols, width)
        normed = layer_norm(x)
        g = dot3(normed, gate_w)
        u = dot3(normed, up_w)
        hidden = g / (1.0 + jnp.exp(-g)) * u
        mid = x + dot3(hidden, out_w)
        mid_v[first * cols:(first + part) * cols] = mid
        tiles = part // cols
        halves = mid.reshape(tiles, 2, packed, width)
        both = jnp.concatenate([halves[:, 0].reshape(tiles * packed, width), halves[:, 1].reshape(tiles * packed, width)], axis=1)
        k0 = first // cols
        sbuf[k0:k0 + tiles, :packed, :] = dot3(both, wide_w).reshape(tiles, packed, 2 * bins)
        lax.fori_loop(k0, k0 + tiles, send_proj, 0)
        dests = part // tok
        norm_mid = layer_norm(mid).reshape(dests, tok, cols, width)
        quad = jnp.concatenate([norm_mid[:, q].reshape(dests * cols, width) for q in range(tok)], axis=1)
        d0 = first // tok
        bsend[d0:d0 + dests] = dot3(quad, bias_w).reshape(dests, cols, lanes)
        lax.fori_loop(d0, d0 + dests, send_bias, 0)
        proj_v[first * cols:(first + part) * cols] = dot3(mid, dist_w)

    brecv[c] = bsend[c]

    @pl.when(p_row == r)
    def _():
        rbuf[p_slot] = sbuf[p_slot]

    for load in loads[8:]:
        load.wait()

    def drain(ref, count, sem):
        pltpu.make_async_copy(ref.at[pl.ds(0, count)], ref.at[pl.ds(0, count)], sem).wait()

    drain(gath, n_dev - 1, g_recv)
    step = 8 // tok
    for m in range(n_dev // step):
        tokens[m * 8:(m + 1) * 8, :] = jnp.concatenate([gath[m * step + q] for q in range(step)], axis=0)
    everyone = layer_norm(tokens[:, :single_width])
    key = dot3(everyone, wk_v[...])
    value = dot3(everyone, wv_v[...])
    slots = lanes // heads
    own = jnp.concatenate([single_v[...], jnp.zeros((slots - tok, single_width), F32)], axis=0)
    own_norm = layer_norm(own)
    query = dot3(own_norm, wq_v[...])
    gating = jax.nn.sigmoid(dot3(own_norm, wg_v[...]))
    head_mask = (iota((heads, single_width), 1) // head_dim == iota((heads, single_width), 0)).astype(F32)
    query_wide = (query[:, None, :] * head_mask[None]).reshape(lanes, single_width)
    scores = dot3(key, query_wide, NT) * (1.0 / head_dim ** 0.5)
    pads = tokens[:, single_width:]

    drain(brecv, n_col - 1, b_recv)
    scores = scores + brecv[...].reshape(scores.shape)
    scores = jnp.where(pads > 0.5, scores, -1e9)
    expo = jnp.exp(scores - jnp.max(scores, axis=0, keepdims=True))
    weights = expo / jnp.sum(expo, axis=0, keepdims=True)
    mixed = dot3(jnp.transpose(weights), value).reshape(slots, heads, single_width)
    attended = jnp.sum(mixed * head_mask[None], axis=1)
    single_o[...] = (own + dot3(gating * attended, wo_v[...]))[:tok]

    @pl.when(p_row == r)
    def _():
        drain(rbuf, group - 1, p_recv)

    @pl.when(p_row != r)
    def _():
        drain(rbuf, group, p_recv)

    half = cols // 2
    for q in range(cols):
        piece = rbuf[:, pl.ds(q, half, stride=cols), :]
        flip_v[:, q] = jnp.concatenate([piece[:, :, :bins], piece[:, :, bins:]], axis=1)
    total = rows * cols
    logits = proj_v[...] + flip_v[...].reshape(total, bins) + bdist_v[...]
    expo = jnp.exp(logits - jnp.max(logits, axis=-1, keepdims=True))
    probs = expo / jnp.sum(expo, axis=-1, keepdims=True)
    ones = jnp.ones((cols, bins), BF16)
    lane = iota((rows, cols, cols), 2)
    mine = jnp.broadcast_to(target_v[...].astype(F32)[:, None, :], (rows, cols, cols))
    mine = jnp.where(lane == iota((rows, cols, cols), 1), mine, 0.0).reshape(total, cols)
    mine = mm(mine.astype(BF16), ones)
    theirs = jnp.broadcast_to(rbuf[:, packed:, :cols][:, None], (group, cols, cols, cols))
    fours = (group, cols, cols, cols)
    theirs = jnp.where(iota(fours, 3) == iota(fours, 1), theirs, 0.0).reshape(total, cols)
    theirs = mm(theirs.astype(BF16), ones)
    bin_id = iota((total, bins), 1).astype(F32)
    hot = (mine == bin_id).astype(F32) + (theirs == bin_id).astype(F32)
    pad_i = tokens[pl.ds(pl.multiple_of(r * rows, rows), rows), single_width:single_width + bins]
    pad_j = tokens[pl.ds(pl.multiple_of(c * cols, cols), cols), single_width:single_width + bins]
    mask = (pad_i[:, None, :] * pad_j[None, :, :]).reshape(total, bins)
    delta = mask * (2.0 * probs - hot)
    pair_o[...] = (mid_v[...] + dot3(delta, dist_w, NT)).reshape(rows, cols, width)

    drain(gath, n_dev - 1, g_send)
    drain(brecv, n_col - 1, b_send)

    @pl.when(p_row == r)
    def _():
        drain(rbuf, group - 1, p_send)

    @pl.when(p_row != r)
    def _():
        drain(rbuf, group, p_send)


def per_device(n_row, n_col, pair, single, target_bins, token_pad, *weights):
    rows, cols, width = pair.shape
    tok, single_width = single.shape
    w_gate, w_up, w_out, w_bias, w_query, w_key, w_value, w_gating, w_attn_out, w_dist, b_dist = weights
    heads = w_bias.shape[1]
    bins = w_dist.shape[1]
    n_dev = n_row * n_col
    lanes = -(-tok * heads // 128) * 128
    group = rows // cols
    packed = cols * cols // 2
    b_dist = b_dist.reshape(1, bins)
    arrays = (pair, single, target_bins, token_pad, w_gate, w_up, w_out, w_bias, w_query, w_key, w_value, w_gating,
              w_attn_out, w_dist, b_dist)
    anywhere = pl.BlockSpec(memory_space=pl.ANY)
    vmem = pl.BlockSpec(memory_space=pltpu.VMEM)
    in_specs = [pl.BlockSpec(memory_space=pltpu.SMEM) if k == 3 else anywhere for k in range(len(arrays))]
    local = [pltpu.VMEM(a.shape, a.dtype) for k, a in enumerate(arrays) if k != 3]
    dma = pltpu.SemaphoreType.DMA
    return pl.pallas_call(
        functools.partial(kernel, n_row, n_col, heads),
        out_shape=(jax.ShapeDtypeStruct(pair.shape, F32), jax.ShapeDtypeStruct(single.shape, F32)),
        in_specs=in_specs,
        out_specs=(vmem, vmem),
        scratch_shapes=local + [
            pltpu.VMEM((tok, single_width + 128), F32),
            pltpu.VMEM((n_dev, tok, single_width + 128), F32),
            pltpu.VMEM((n_dev * tok, single_width + 128), F32),
            pltpu.VMEM((rows * cols, width), F32),
            pltpu.VMEM((rows * cols, bins), F32),
            pltpu.VMEM((group, cols, cols, bins), F32),
            pltpu.VMEM((group, packed + cols, 128), F32),
            pltpu.VMEM((group, packed + cols, 128), F32),
            pltpu.VMEM((n_col, cols, lanes), F32),
            pltpu.VMEM((n_col, cols, lanes), F32),
            dma((len(arrays) - 1,)), dma, dma, dma, dma, dma, dma,
        ],
        compiler_params=pltpu.CompilerParams(
            collective_id=0, has_side_effects=True, vmem_limit_bytes=56 * 2**20
        ),
        name="pairformer_close",
    )(*arrays)


def solution(mesh):
    in_specs = (
        P("row", "col", None),
        P(("row", "col"), None),
        P("row", "col"),
        P(("row", "col")),
    ) + (P(),) * 11
    out_specs = (P("row", "col", None), P(("row", "col"), None))
    body = functools.partial(per_device, mesh.shape["row"], mesh.shape["col"])
    return jax.shard_map(body, mesh=mesh, in_specs=in_specs, out_specs=out_specs, check_vma=False)
```

time: 260 us -> 29.7 us (0.11)
  blocking collectives: 160 us -> 0 us
  Pallas kernels: 0 us -> 23.7 us
  waiting for transfers between devices: 21.1 us -> 0 us
  starting transfers between devices: 20.8 us -> 0 us
  matrix products: 16.2 us -> 0 us
  between operations: 15.8 us -> 0.66 us
  local copies, waits for them, and re-layouts: 16.9 us -> 5.14 us
  other arithmetic: 6.81 us -> 0 us
    all_gather x7 -> x0, blocking collectives: 109 us -> none  [the longest x2 44 us: joined(): pieces = jax.tree.map(lambda part: lax.all_gather(part, axis), value)]
    unnamed x2 -> x0, blocking collectives: 39.8 us -> none
    pallas_call x0 -> x1, Pallas kernels: none -> 23.7 us  [per_device(): pl.pallas_call(functools.partial(kernel, n_row, n_col, heads), out_shape=...]
    all_to_all x6 -> x0, waiting for transfers between devices: 21 us -> none  [the longest x1 6.61 us: per_device(): lax.all_to_all(lax.all_to_all(to_blocks(proj_rows, bins), 'row', split_ax...]
    all_to_all x6 -> x0, starting transfers between devices: 20.8 us -> none  [the longest x1 3.51 us: per_device(): lax.all_to_all(lax.all_to_all(to_blocks(proj_rows, bins), 'row', split_ax...]
    dot_general x28 -> x0, matrix products: 16.2 us -> none  [the longest x26 14.6 us: dense(): out = jnp.dot(flat, w, precision=HI, preferred_element_type=jnp.float32)]
    all_to_all x1 -> x0, blocking collectives: 10.8 us -> none  [per_device(): lax.all_to_all(proj, 'col', split_axis=0, concat_axis=1, tiled=True)]
    reduce_sum x20 -> x0, other arithmetic: 3.95 us -> none  [the longest x9 2.14 us: layer_norm(): var = jnp.mean(centred * centred, axis=-1, keepdims=True)]
  transfers between devices with their start and end apart: 7 -> 0, of which waited for: 4 -> 0; matrix products, arithmetic and copies ran while one was open for 4% -> 0% of each run, Pallas kernels for 0% -> 0%
where the time goes in v1:
time: 29.7 us; the launch traced here: 29.5 us
  Pallas kernels  23.7 us (80%)
  local copies, waits for them, and re-layouts  5.14 us (17%)
  between operations  0.66 us (2%)
    pallas_call x1, Pallas kernels, per_device(): pl.pallas_call(functools.partial(kernel, n_row, n_col, heads), out_shape=...  23.7 us
    unnamed x11, local copies, waits for them, and re-layouts  5.14 us

profile of v1, /device:TPU:0, one launch (start us, length us, event | category | flops | bytes accessed | tf_op | source)
XLA Modules:
  0.0 29.5 jit_solution(6785415364420676025)
XLA Ops:
  0.6 0.0 copy-start.1
  0.6 1.4 %copy.17.refs_2_ = s32[64,8]{1,0:T(8,128)} copy(s32[64,8]{0,1:T(8,128)} %param.17) | data formatting | bytes 4096 | tf_op args[2]
  2.0 0.0 copy-done.1
  2.0 0.0 copy-start
  2.0 0.7 %copy.18.refs_7_ = f32[128,16]{1,0:T(8,128)} copy(f32[128,16]{0,1:T(8,128)S(1)} %copy-done.1) | data formatting | bytes 16384 | tf_op args[7]
  2.7 0.0 copy-done
  2.8 0.7 %copy.19.refs_13_ = f32[128,64]{1,0:T(8,128)} copy(f32[128,64]{0,1:T(8,128)S(1)} %copy-done) | data formatting | bytes 65536 | tf_op args[13]
  3.5 23.7 %pairformer_close.1 = (f32[64,8,128]{2,1,0:T(8,128)}, f32[4,384]{1,0:T(4,128)}) custom-call(f32[64,8,128]{2,1,0:T(8,128)} %refs_0_.1, f32[4,384]{1,0:T(4,128)} %refs_1_.1, s32[64,8]{1,0:T(8,128)} %copy.17.refs_2_, s32[4]{0:T(128)} %refs_3_.1, f32[128,512]{1,0:T(8,128)} %refs_4_.1, f32[128,512]{1,0:T(8,128)} %refs_5_.1, f32[512,128]{1,0:T(8,128)} %refs_6_.1, ...), custom_call_target="tpu_custom_call" | custom-call | tf_op jit(solution)/shard_map/pairformer_close/pallas_call | solution.py:258
  27.2 0.0 copy-start.2
  27.2 1.7 %copy.22 = f32[64,8,128]{2,1,0:T(8,128)} copy(f32[64,8,128]{2,1,0:T(8,128)} %get-tuple-element.4) | data formatting | bytes 524288
  28.9 0.0 copy-done.2
  28.9 0.6 %copy.23 = f32[4,384]{1,0:T(4,128)} copy(f32[4,384]{1,0:T(4,128)S(1)} %copy-done.2) | data formatting | bytes 12288
Async XLA Ops:
  0.6 1.4 %copy-start.1 = (f32[128,16]{0,1:T(8,128)S(1)}, f32[128,16]{0,1:T(8,128)}, u32[]{:S(2)}) copy-start(f32[128,16]{0,1:T(8,128)} %param.22) | copy-start | bytes 24580
  2.0 0.8 %copy-start = (f32[128,64]{0,1:T(8,128)S(1)}, f32[128,64]{0,1:T(8,128)}, u32[]{:S(2)}) copy-start(f32[128,64]{0,1:T(8,128)} %param.28) | copy-start | bytes 98308
  27.2 1.7 %copy-start.2 = (f32[4,384]{1,0:T(4,128)S(1)}, f32[4,384]{1,0:T(4,128)}, u32[]{:S(2)}) copy-start(f32[4,384]{1,0:T(4,128)} %get-tuple-element.5) | copy-start | bytes 18436

commit v2 on v1

--- a/solution.py
+++ b/solution.py
@@ -49,15 +49,13 @@
      in_sem, g_send, g_recv, b_send, b_recv, p_send, p_recv) = refs
     rows, cols, width = pair_v.shape
     tok, single_width = single_v.shape
-    bins = wdist_v.shape[1]
-    n_dev = n_row * n_col
+    bins = wdist_v.shape[0]
     group = rows // cols
     lanes = bsend.shape[2]
     head_dim = single_width // heads
     packed = cols * cols // 2
     r = lax.axis_index("row")
     c = lax.axis_index("col")
-    me = r * n_col + c
 
     sources = (single_h, pair_h, gate_h, up_h, wout_h, target_h, wbias_h, wdist_h, wk_h, wv_h, wq_h, wg_h, wo_h, bdist_h)
     targets = (single_v, pair_v, gate_v, up_v, wout_v, target_v, wbias_v, wdist_v, wk_v, wv_v, wq_v, wg_v, wo_v, bdist_v)
@@ -65,17 +63,29 @@
     for load in loads:
         load.start()
 
+    chip, core = c // 2, lax.rem(c, 2)
+    chips = n_col // 2
+    p_row = c // group
+    p_slot = lax.rem(c, group)
+    at_home = p_row == r
+
+    def is_self(k):
+        return jnp.logical_and(at_home, p_slot == k)
+
     barrier = pltpu.get_barrier_semaphore()
 
-    def other(step):
-        d = lax.rem(me + step, n_dev)
-        return d // n_col, lax.rem(d, n_col)
-
-    def greet(step, carry):
-        pl.semaphore_signal(barrier, inc=1, device_id=other(step), device_id_type=MESH)
-        return carry
-
-    lax.fori_loop(1, n_dev, greet, 0)
+    def greet(row, col):
+        pl.semaphore_signal(barrier, inc=1, device_id=(row, col), device_id_type=MESH)
+
+    for step in range(1, n_col):
+        greet(r, lax.rem(c + step, n_col))
+    for step in range(1, n_row):
+        greet(lax.rem(r + step, n_row), c)
+
+    @pl.when(jnp.logical_not(at_home))
+    def _():
+        for k in range(group):
+            greet(p_row, group * r + k)
 
     loads[0].wait()
     row_id = iota((tok, 128), 0)
@@ -84,14 +94,11 @@
         pad_tile = jnp.where(row_id == q, pad_s[q].astype(F32), pad_tile)
     ext[:, :single_width] = single_v[...]
     ext[:, single_width:] = pad_tile
-    gath[me] = ext[...]
-    pl.semaphore_wait(barrier, n_dev - 1)
-
-    def share(step, carry):
-        pltpu.make_async_remote_copy(ext, gath.at[me], g_send, g_recv, device_id=other(step), device_id_type=MESH).start()
-        return carry
-
-    lax.fori_loop(1, n_dev, share, 0)
+    gath[chip, core, r] = ext[...]
+    pl.semaphore_wait(barrier, n_col + n_row - 2 + jnp.where(at_home, 0, group))
+
+    for step in range(1, n_row):
+        pltpu.make_async_remote_copy(ext, gath.at[chip, core, r], g_send.at[0], g_recv.at[0], device_id=(lax.rem(r + step, n_row), c), device_id_type=MESH).start()
 
     for load in loads[1:8]:
         load.wait()
@@ -104,26 +111,30 @@
     none = jnp.zeros_like(wdist)
     wide = jnp.concatenate([jnp.concatenate([wdist, none], axis=1), jnp.concatenate([none, wdist], axis=1)], axis=0)
     wide_w = split(wide)
-    spread = (iota((heads, lanes), 0) == lax.rem(iota((heads, lanes), 1), heads)).astype(F32)
-    bias_rep = lax.dot_general(wbias_v[...], spread, NN, precision=lax.Precision.HIGHEST, preferred_element_type=F32)
-    lane_q = iota((width, lanes), 1) // heads
-    bias_w = split(jnp.concatenate([jnp.where(lane_q == q, bias_rep, 0.0) for q in range(tok)], axis=0))
-
-    sbuf[:, packed:, :] = jnp.zeros((group, cols, 128), F32)
-    sbuf[:, packed:, :cols] = target_v[...].astype(F32).reshape(group, cols, cols)
+    slots = lanes // heads
+    bias_rep = jnp.concatenate([wbias_v[...]] * slots, axis=0)
+    row_q = iota((lanes, width), 0) // heads
+    bias_w = split(jnp.concatenate([jnp.where(row_q == q, bias_rep, 0.0) for q in range(tok)], axis=1))
+
+    bin_rows = target_v[...].astype(F32)
+    eye = (iota((rows, rows), 0) == iota((rows, rows), 1)).astype(BF16)
+    filled = jnp.concatenate([bin_rows, jnp.zeros((128 - cols, rows), F32)], axis=0).astype(BF16)
+    sbuf[:, packed:, :] = mm(eye, filled, NT).reshape(group, cols, 128)
+
+    def drain(ref, sem):
+        pltpu.make_async_copy(ref, ref, sem).wait()
+
+    drain(gath.at[0, 0, pl.ds(0, n_row - 1)], g_recv.at[0])
+    for step in range(1, chips):
+        pltpu.make_async_remote_copy(gath.at[chip, core], gath.at[chip, core], g_send.at[1], g_recv.at[1], device_id=(r, lax.rem(c + 2 * step, n_col)), device_id_type=MESH).start()
 
     part = rows // PARTS
-    p_row = c // group
-    p_slot = lax.rem(c, group)
 
     def send_bias(d, carry):
         @pl.when(d != c)
         def _():
             pltpu.make_async_remote_copy(bsend.at[d], brecv.at[c], b_send, b_recv, device_id=(r, d), device_id_type=MESH).start()
         return carry
-
-    def is_self(k):
-        return jnp.logical_and(p_row == r, p_slot == k)
 
     def send_proj(k, carry):
         @pl.when(jnp.logical_not(is_self(k)))
@@ -144,15 +155,18 @@
         halves = mid.reshape(tiles, 2, packed, width)
         both = jnp.concatenate([halves[:, 0].reshape(tiles * packed, width), halves[:, 1].reshape(tiles * packed, width)], axis=1)
         k0 = first // cols
-        sbuf[k0:k0 + tiles, :packed, :] = dot3(both, wide_w).reshape(tiles, packed, 2 * bins)
+        sbuf[k0:k0 + tiles, :packed, :] = dot3(both, wide_w, NT).reshape(tiles, packed, 2 * bins)
         lax.fori_loop(k0, k0 + tiles, send_proj, 0)
         dests = part // tok
         norm_mid = layer_norm(mid).reshape(dests, tok, cols, width)
         quad = jnp.concatenate([norm_mid[:, q].reshape(dests * cols, width) for q in range(tok)], axis=1)
         d0 = first // tok
-        bsend[d0:d0 + dests] = dot3(quad, bias_w).reshape(dests, cols, lanes)
+        bsend[d0:d0 + dests] = dot3(quad, bias_w, NT).reshape(dests, cols, lanes)
         lax.fori_loop(d0, d0 + dests, send_bias, 0)
-        proj_v[first * cols:(first + part) * cols] = dot3(mid, dist_w)
+        proj_v[first * cols:(first + part) * cols] = dot3(mid, dist_w, NT)
+        if s == 0:
+            drain(gath.at[pl.ds(0, chips - 1), 0], g_recv.at[1])
+            pltpu.make_async_remote_copy(gath.at[:, core], gath.at[:, core], g_send.at[2], g_recv.at[2], device_id=(r, c + 1 - 2 * core), device_id_type=MESH).start()
 
     brecv[c] = bsend[c]
 
@@ -163,17 +177,15 @@
     for load in loads[8:]:
         load.wait()
 
-    def drain(ref, count, sem):
-        pltpu.make_async_copy(ref.at[pl.ds(0, count)], ref.at[pl.ds(0, count)], sem).wait()
-
-    drain(gath, n_dev - 1, g_recv)
+    drain(gath.at[:, 0], g_recv.at[2])
     step = 8 // tok
-    for m in range(n_dev // step):
-        tokens[m * 8:(m + 1) * 8, :] = jnp.concatenate([gath[m * step + q] for q in range(step)], axis=0)
+    for row in range(n_row):
+        for m in range(0, n_col, step):
+            at = (row * n_col + m) * tok
+            tokens[at:at + 8, :] = jnp.concatenate([gath[(m + q) // 2, (m + q) % 2, row] for q in range(step)], axis=0)
     everyone = layer_norm(tokens[:, :single_width])
     key = dot3(everyone, wk_v[...])
     value = dot3(everyone, wv_v[...])
-    slots = lanes // heads
     own = jnp.concatenate([single_v[...], jnp.zeros((slots - tok, single_width), F32)], axis=0)
     own_norm = layer_norm(own)
     query = dot3(own_norm, wq_v[...])
@@ -183,7 +195,7 @@
     scores = dot3(key, query_wide, NT) * (1.0 / head_dim ** 0.5)
     pads = tokens[:, single_width:]
 
-    drain(brecv, n_col - 1, b_recv)
+    drain(brecv.at[pl.ds(0, n_col - 1)], b_recv)
     scores = scores + brecv[...].reshape(scores.shape)
     scores = jnp.where(pads > 0.5, scores, -1e9)
     expo = jnp.exp(scores - jnp.max(scores, axis=0, keepdims=True))
@@ -194,11 +206,11 @@
 
     @pl.when(p_row == r)
     def _():
-        drain(rbuf, group - 1, p_recv)
+        drain(rbuf.at[pl.ds(0, group - 1)], p_recv)
 
     @pl.when(p_row != r)
     def _():
-        drain(rbuf, group, p_recv)
+        drain(rbuf, p_recv)
 
     half = cols // 2
     for q in range(cols):
@@ -209,10 +221,9 @@
     expo = jnp.exp(logits - jnp.max(logits, axis=-1, keepdims=True))
     probs = expo / jnp.sum(expo, axis=-1, keepdims=True)
     ones = jnp.ones((cols, bins), BF16)
-    lane = iota((rows, cols, cols), 2)
-    mine = jnp.broadcast_to(target_v[...].astype(F32)[:, None, :], (rows, cols, cols))
-    mine = jnp.where(lane == iota((rows, cols, cols), 1), mine, 0.0).reshape(total, cols)
-    mine = mm(mine.astype(BF16), ones)
+    three = (rows, cols, rows)
+    mine = jnp.where(iota(three, 2) == iota(three, 0), jnp.broadcast_to(bin_rows[None], three), 0.0).reshape(total, rows)
+    mine = mm(mine.astype(BF16), jnp.ones((rows, bins), BF16))
     theirs = jnp.broadcast_to(rbuf[:, packed:, :cols][:, None], (group, cols, cols, cols))
     fours = (group, cols, cols, cols)
     theirs = jnp.where(iota(fours, 3) == iota(fours, 1), theirs, 0.0).reshape(total, cols)
@@ -223,18 +234,20 @@
     pad_j = tokens[pl.ds(pl.multiple_of(c * cols, cols), cols), single_width:single_width + bins]
     mask = (pad_i[:, None, :] * pad_j[None, :, :]).reshape(total, bins)
     delta = mask * (2.0 * probs - hot)
-    pair_o[...] = (mid_v[...] + dot3(delta, dist_w, NT)).reshape(rows, cols, width)
-
-    drain(gath, n_dev - 1, g_send)
-    drain(brecv, n_col - 1, b_send)
+    pair_o[...] = (mid_v[...] + dot3(delta, dist_w)).reshape(rows, cols, width)
+
+    drain(gath.at[0, 0, pl.ds(0, n_row - 1)], g_send.at[0])
+    drain(gath.at[pl.ds(0, chips - 1), 0], g_send.at[1])
+    drain(gath.at[:, 0], g_send.at[2])
+    drain(brecv.at[pl.ds(0, n_col - 1)], b_send)
 
     @pl.when(p_row == r)
     def _():
-        drain(rbuf, group - 1, p_send)
+        drain(rbuf.at[pl.ds(0, group - 1)], p_send)
 
     @pl.when(p_row != r)
     def _():
-        drain(rbuf, group, p_send)
+        drain(rbuf, p_send)
 
 
 def per_device(n_row, n_col, pair, single, target_bins, token_pad, *weights):
@@ -243,6 +256,7 @@
     w_gate, w_up, w_out, w_bias, w_query, w_key, w_value, w_gating, w_attn_out, w_dist, b_dist = weights
     heads = w_bias.shape[1]
     bins = w_dist.shape[1]
+    w_bias, w_dist, target_bins = w_bias.T, w_dist.T, target_bins.T
     n_dev = n_row * n_col
     lanes = -(-tok * heads // 128) * 128
     group = rows // cols
@@ -262,7 +276,7 @@
         out_specs=(vmem, vmem),
         scratch_shapes=local + [
             pltpu.VMEM((tok, single_width + 128), F32),
-            pltpu.VMEM((n_dev, tok, single_width + 128), F32),
+            pltpu.VMEM((n_col // 2, 2, n_row, tok, single_width + 128), F32),
             pltpu.VMEM((n_dev * tok, single_width + 128), F32),
             pltpu.VMEM((rows * cols, width), F32),
             pltpu.VMEM((rows * cols, bins), F32),
@@ -271,7 +285,7 @@
             pltpu.VMEM((group, packed + cols, 128), F32),
             pltpu.VMEM((n_col, cols, lanes), F32),
             pltpu.VMEM((n_col, cols, lanes), F32),
-            dma((len(arrays) - 1,)), dma, dma, dma, dma, dma, dma,
+            dma((len(arrays) - 1,)), dma((3,)), dma((3,)), dma, dma, dma, dma,
         ],
         compiler_params=pltpu.CompilerParams(
             collective_id=0, has_side_effects=True, vmem_limit_bytes=56 * 2**20

time: 29.7 us -> 25.8 us (0.87)
  local copies, waits for them, and re-layouts: 5.14 us -> 2.27 us
  Pallas kernels: 23.7 us -> 22.7 us
    unnamed x11 -> x4, local copies, waits for them, and re-layouts: 5.14 us -> 2.27 us
    pallas_call x1, Pallas kernels: 23.7 us -> 22.7 us  [per_device(): pl.pallas_call(functools.partial(kernel, n_row, n_col, heads), out_shape=...]
where the time goes in v2:
time: 25.8 us; the launch traced here: 25.6 us
  Pallas kernels  22.7 us (88%)
  local copies, waits for them, and re-layouts  2.27 us (9%)
  between operations  0.65 us (3%)
    pallas_call x1, Pallas kernels, per_device(): pl.pallas_call(functools.partial(kernel, n_row, n_col, heads), out_shape=...  22.7 us
    unnamed x4, local copies, waits for them, and re-layouts  2.27 us

profile of v2, /device:TPU:0, one launch (start us, length us, event | category | flops | bytes accessed | tf_op | source)
XLA Modules:
  0.0 25.6 jit_solution(9687145352599351833)
XLA Ops:
  0.6 22.7 %pairformer_close.1 = (f32[64,8,128]{2,1,0:T(8,128)}, f32[4,384]{1,0:T(4,128)}) custom-call(f32[64,8,128]{2,1,0:T(8,128)} %refs_0_.1, f32[4,384]{1,0:T(4,128)} %refs_1_.1, s32[8,64]{1,0:T(8,128)} %bitcast.6, s32[4]{0:T(128)} %refs_3_.1, f32[128,512]{1,0:T(8,128)} %refs_4_.1, f32[128,512]{1,0:T(8,128)} %refs_5_.1, f32[512,128]{1,0:T(8,128)} %refs_6_.1, ...), custom_call_target="tpu_custom_call" | custom-call | tf_op jit(solution)/shard_map/pairformer_close/pallas_call | solution.py:272
  23.3 0.0 copy-start
  23.3 1.7 %copy.19 = f32[64,8,128]{2,1,0:T(8,128)} copy(f32[64,8,128]{2,1,0:T(8,128)} %get-tuple-element.4) | data formatting | bytes 524288
  25.0 0.0 copy-done
  25.0 0.6 %copy.20 = f32[4,384]{1,0:T(4,128)} copy(f32[4,384]{1,0:T(4,128)S(1)} %copy-done) | data formatting | bytes 12288
Async XLA Ops:
  23.3 1.7 %copy-start = (f32[4,384]{1,0:T(4,128)S(1)}, f32[4,384]{1,0:T(4,128)}, u32[]{:S(2)}) copy-start(f32[4,384]{1,0:T(4,128)} %get-tuple-element.5) | copy-start | bytes 18436

commit v3 on v2

--- a/solution.py
+++ b/solution.py
@@ -27,7 +27,12 @@
 def dot3(a, b, dims=NN):
     ah, al = split(a)
     bh, bl = b if isinstance(b, tuple) else split(b)
-    return mm(ah, bh, dims) + (mm(al, bh, dims) + mm(ah, bl, dims))
+    rows = a.shape[0]
+    if rows % 16:
+        both = mm(jnp.concatenate([ah.astype(F32), al.astype(F32)], axis=0).astype(BF16), bh, dims)
+    else:
+        both = mm(jnp.concatenate([ah, al], axis=0), bh, dims)
+    return both[:rows] + (both[rows:] + mm(ah, bl, dims))
 
 
 def layer_norm(x):
@@ -250,6 +255,15 @@
         drain(rbuf, p_send)
 
 
+def hand_over(pair_in, single_in, pair_out, single_out, pair_sem, single_sem):
+    first = pltpu.make_async_copy(pair_in, pair_out, pair_sem)
+    second = pltpu.make_async_copy(single_in, single_out, single_sem)
+    first.start()
+    second.start()
+    first.wait()
+    second.wait()
+
+
 def per_device(n_row, n_col, pair, single, target_bins, token_pad, *weights):
     rows, cols, width = pair.shape
     tok, single_width = single.shape
@@ -269,9 +283,9 @@
     in_specs = [pl.BlockSpec(memory_space=pltpu.SMEM) if k == 3 else anywhere for k in range(len(arrays))]
     local = [pltpu.VMEM(a.shape, a.dtype) for k, a in enumerate(arrays) if k != 3]
     dma = pltpu.SemaphoreType.DMA
-    return pl.pallas_call(
+    results = pl.pallas_call(
         functools.partial(kernel, n_row, n_col, heads),
-        out_shape=(jax.ShapeDtypeStruct(pair.shape, F32), jax.ShapeDtypeStruct(single.shape, F32)),
+        out_shape=(pltpu.VMEM(pair.shape, F32), pltpu.VMEM(single.shape, F32)),
         in_specs=in_specs,
         out_specs=(vmem, vmem),
         scratch_shapes=local + [
@@ -292,6 +306,14 @@
         ),
         name="pairformer_close",
     )(*arrays)
+    return pl.pallas_call(
+        hand_over,
+        out_shape=(jax.ShapeDtypeStruct(pair.shape, F32), jax.ShapeDtypeStruct(single.shape, F32)),
+        in_specs=[vmem, vmem],
+        out_specs=(anywhere, anywhere),
+        scratch_shapes=[dma, dma],
+        name="hand_over",
+    )(*results)
 
 
 def solution(mesh):

time: 25.8 us -> 25.7 us (level)
  local copies, waits for them, and re-layouts: 2.27 us -> 1.27 us
  Pallas kernels: 22.7 us -> 23.6 us
    pallas_call x0 -> x1, Pallas kernels: none -> 1.67 us  [per_device(): pl.pallas_call(hand_over, out_shape=(jax.ShapeDtypeStruct(pair.shape, F32...]
    unnamed x4, local copies, waits for them, and re-layouts: 2.27 us -> 1.27 us
    pallas_call x1, Pallas kernels: 22.7 us -> 21.9 us  [per_device(): pl.pallas_call(functools.partial(kernel, n_row, n_col, heads), out_shape=...]
where the time goes in v3:
time: 25.7 us; the launch traced here: 25.5 us
  Pallas kernels  23.6 us (92%)
  local copies, waits for them, and re-layouts  1.27 us (5%)
  between operations  0.65 us (3%)
    pallas_call x1, Pallas kernels, per_device(): pl.pallas_call(functools.partial(kernel, n_row, n_col, heads), out_shape=...  21.9 us
    pallas_call x1, Pallas kernels, per_device(): pl.pallas_call(hand_over, out_shape=(jax.ShapeDtypeStruct(pair.shape, F32...  1.67 us
    unnamed x4, local copies, waits for them, and re-layouts  1.27 us

profile of v3, /device:TPU:0, one launch (start us, length us, event | category | flops | bytes accessed | tf_op | source)
XLA Modules:
  0.0 25.5 jit_solution(7306438267166265520)
XLA Ops:
  0.6 21.9 %pairformer_close.1 = (f32[64,8,128]{2,1,0:T(8,128)S(1)}, f32[4,384]{1,0:T(4,128)S(1)}) custom-call(f32[64,8,128]{2,1,0:T(8,128)} %refs_0_.1, f32[4,384]{1,0:T(4,128)} %refs_1_.1, s32[8,64]{1,0:T(8,128)} %bitcast.6, s32[4]{0:T(128)} %refs_3_.1, f32[128,512]{1,0:T(8,128)} %refs_4_.1, f32[128,512]{1,0:T(8,128)} %refs_5_.1, f32[512,128]{1,0:T(8,128)} %refs_6_.1, ...), custom_call_target="tpu_custom_call" | custom-call | tf_op jit(solution)/shard_map/pairformer_close/pallas_call | solution.py:286
  22.6 0.0 copy-start
  22.6 0.7 %copy-done = f32[64,8,128]{2,1,0:T(8,128)} copy-done((f32[64,8,128]{2,1,0:T(8,128)}, f32[64,8,128]{2,1,0:T(8,128)S(1)}, u32[]{:S(2)}) %copy-start) | copy-done | bytes 262168
  23.3 0.0 copy-start.1
  23.3 0.6 %copy-done.1 = f32[4,384]{1,0:T(4,128)} copy-done((f32[4,384]{1,0:T(4,128)}, f32[4,384]{1,0:T(4,128)S(1)}, u32[]{:S(2)}) %copy-start.1) | copy-done | bytes 6168
  23.8 1.7 %hand_over.1 = (f32[64,8,128]{2,1,0:T(8,128)}, f32[4,384]{1,0:T(4,128)}) custom-call(f32[64,8,128]{2,1,0:T(8,128)} %copy-done, f32[4,384]{1,0:T(4,128)} %copy-done.1), custom_call_target="tpu_custom_call" | custom-call | tf_op jit(solution)/shard_map/hand_over/pallas_call | solution.py:309
Async XLA Ops:
  22.6 0.7 %copy-start = (f32[64,8,128]{2,1,0:T(8,128)}, f32[64,8,128]{2,1,0:T(8,128)S(1)}, u32[]{:S(2)}) copy-start(f32[64,8,128]{2,1,0:T(8,128)S(1)} %get-tuple-element.4.pair_in) | copy-start | bytes 786436
  23.3 0.6 %copy-start.1 = (f32[4,384]{1,0:T(4,128)}, f32[4,384]{1,0:T(4,128)S(1)}, u32[]{:S(2)}) copy-start(f32[4,384]{1,0:T(4,128)S(1)} %get-tuple-element.5.single_in) | copy-start | bytes 18436

commit v4 on v2

--- a/solution.py
+++ b/solution.py
@@ -12,7 +12,7 @@
 BF16 = jnp.bfloat16
 NN = (((1,), (0,)), ((), ()))
 NT = (((1,), (1,)), ((), ()))
-PARTS = 2
+PARTS = 4
 
 
 def split(x):
@@ -27,7 +27,12 @@
 def dot3(a, b, dims=NN):
     ah, al = split(a)
     bh, bl = b if isinstance(b, tuple) else split(b)
-    return mm(ah, bh, dims) + (mm(al, bh, dims) + mm(ah, bl, dims))
+    rows = a.shape[0]
+    if rows % 16:
+        both = mm(jnp.concatenate([ah.astype(F32), al.astype(F32)], axis=0).astype(BF16), bh, dims)
+    else:
+        both = mm(jnp.concatenate([ah, al], axis=0), bh, dims)
+    return both[:rows] + (both[rows:] + mm(ah, bl, dims))
 
 
 def layer_norm(x):
@@ -124,10 +129,6 @@
     def drain(ref, sem):
         pltpu.make_async_copy(ref, ref, sem).wait()
 
-    drain(gath.at[0, 0, pl.ds(0, n_row - 1)], g_recv.at[0])
-    for step in range(1, chips):
-        pltpu.make_async_remote_copy(gath.at[chip, core], gath.at[chip, core], g_send.at[1], g_recv.at[1], device_id=(r, lax.rem(c + 2 * step, n_col)), device_id_type=MESH).start()
-
     part = rows // PARTS
 
     def send_bias(d, carry):
@@ -149,7 +150,9 @@
         g = dot3(normed, gate_w)
         u = dot3(normed, up_w)
         hidden = g / (1.0 + jnp.exp(-g)) * u
-        mid = x + dot3(hidden, out_w)
+        change = dot3(hidden, out_w)
+        pair_o[first * cols:(first + part) * cols] = change
+        mid = x + change
         mid_v[first * cols:(first + part) * cols] = mid
         tiles = part // cols
         halves = mid.reshape(tiles, 2, packed, width)
@@ -163,8 +166,11 @@
         d0 = first // tok
         bsend[d0:d0 + dests] = dot3(quad, bias_w, NT).reshape(dests, cols, lanes)
         lax.fori_loop(d0, d0 + dests, send_bias, 0)
-        proj_v[first * cols:(first + part) * cols] = dot3(mid, dist_w, NT)
         if s == 0:
+            drain(gath.at[0, 0, pl.ds(0, n_row - 1)], g_recv.at[0])
+            for step in range(1, chips):
+                pltpu.make_async_remote_copy(gath.at[chip, core], gath.at[chip, core], g_send.at[1], g_recv.at[1], device_id=(r, lax.rem(c + 2 * step, n_col)), device_id_type=MESH).start()
+        if s == PARTS // 2:
             drain(gath.at[pl.ds(0, chips - 1), 0], g_recv.at[1])
             pltpu.make_async_remote_copy(gath.at[:, core], gath.at[:, core], g_send.at[2], g_recv.at[2], device_id=(r, c + 1 - 2 * core), device_id_type=MESH).start()
 
@@ -177,6 +183,16 @@
     for load in loads[8:]:
         load.wait()
 
+    own = jnp.concatenate([single_v[...], jnp.zeros((slots - tok, single_width), F32)], axis=0)
+    own_norm = layer_norm(own)
+    query = dot3(own_norm, wq_v[...])
+    gating = jax.nn.sigmoid(dot3(own_norm, wg_v[...]))
+    total = rows * cols
+    proj_v[...] = dot3(mid_v[...], dist_w, NT)
+    ones = jnp.ones((cols, bins), BF16)
+    three = (rows, cols, rows)
+    mine = jnp.where(iota(three, 2) == iota(three, 0), jnp.broadcast_to(bin_rows[None], three), 0.0).reshape(total, rows)
+    mine = mm(mine.astype(BF16), jnp.ones((rows, bins), BF16))
     drain(gath.at[:, 0], g_recv.at[2])
     step = 8 // tok
     for row in range(n_row):
@@ -186,10 +202,6 @@
     everyone = layer_norm(tokens[:, :single_width])
     key = dot3(everyone, wk_v[...])
     value = dot3(everyone, wv_v[...])
-    own = jnp.concatenate([single_v[...], jnp.zeros((slots - tok, single_width), F32)], axis=0)
-    own_norm = layer_norm(own)
-    query = dot3(own_norm, wq_v[...])
-    gating = jax.nn.sigmoid(dot3(own_norm, wg_v[...]))
     head_mask = (iota((heads, single_width), 1) // head_dim == iota((heads, single_width), 0)).astype(F32)
     query_wide = (query[:, None, :] * head_mask[None]).reshape(lanes, single_width)
     scores = dot3(key, query_wide, NT) * (1.0 / head_dim ** 0.5)
@@ -216,14 +228,9 @@
     for q in range(cols):
         piece = rbuf[:, pl.ds(q, half, stride=cols), :]
         flip_v[:, q] = jnp.concatenate([piece[:, :, :bins], piece[:, :, bins:]], axis=1)
-    total = rows * cols
     logits = proj_v[...] + flip_v[...].reshape(total, bins) + bdist_v[...]
     expo = jnp.exp(logits - jnp.max(logits, axis=-1, keepdims=True))
     probs = expo / jnp.sum(expo, axis=-1, keepdims=True)
-    ones = jnp.ones((cols, bins), BF16)
-    three = (rows, cols, rows)
-    mine = jnp.where(iota(three, 2) == iota(three, 0), jnp.broadcast_to(bin_rows[None], three), 0.0).reshape(total, rows)
-    mine = mm(mine.astype(BF16), jnp.ones((rows, bins), BF16))
     theirs = jnp.broadcast_to(rbuf[:, packed:, :cols][:, None], (group, cols, cols, cols))
     fours = (group, cols, cols, cols)
     theirs = jnp.where(iota(fours, 3) == iota(fours, 1), theirs, 0.0).reshape(total, cols)
@@ -234,7 +241,7 @@
     pad_j = tokens[pl.ds(pl.multiple_of(c * cols, cols), cols), single_width:single_width + bins]
     mask = (pad_i[:, None, :] * pad_j[None, :, :]).reshape(total, bins)
     delta = mask * (2.0 * probs - hot)
-    pair_o[...] = (mid_v[...] + dot3(delta, dist_w)).reshape(rows, cols, width)
+    pair_o[...] = pair_o[...] + dot3(delta, dist_w)
 
     drain(gath.at[0, 0, pl.ds(0, n_row - 1)], g_send.at[0])
     drain(gath.at[pl.ds(0, chips - 1), 0], g_send.at[1])
@@ -269,9 +276,9 @@
     in_specs = [pl.BlockSpec(memory_space=pltpu.SMEM) if k == 3 else anywhere for k in range(len(arrays))]
     local = [pltpu.VMEM(a.shape, a.dtype) for k, a in enumerate(arrays) if k != 3]
     dma = pltpu.SemaphoreType.DMA
-    return pl.pallas_call(
+    pair_out, single_out = pl.pallas_call(
         functools.partial(kernel, n_row, n_col, heads),
-        out_shape=(jax.ShapeDtypeStruct(pair.shape, F32), jax.ShapeDtypeStruct(single.shape, F32)),
+        out_shape=(jax.ShapeDtypeStruct((rows * cols, width), F32), jax.ShapeDtypeStruct(single.shape, F32)),
         in_specs=in_specs,
         out_specs=(vmem, vmem),
         scratch_shapes=local + [
@@ -292,6 +299,7 @@
         ),
         name="pairformer_close",
     )(*arrays)
+    return pair + pair_out.reshape(pair.shape), single_out
 
 
 def solution(mesh):

time: 25.8 us -> 25 us (0.969)
  the two profiles are of different devices: /device:TPU:0 before, /device:TPU:25 now
where the time goes in v4:
time: 25 us; the launch traced here: 24.8 us
  Pallas kernels  21.8 us (87%)
  other arithmetic  1.69 us (7%)
  between operations  0.67 us (3%)
  local copies, waits for them, and re-layouts  0.6 us (2%)
    pallas_call x1, Pallas kernels, per_device(): pl.pallas_call(functools.partial(kernel, n_row, n_col, heads), out_shape=...  21.8 us
    add x1, other arithmetic, per_device(): return (pair + pair_out.reshape(pair.shape), single_out)  1.69 us
    unnamed x5, local copies, waits for them, and re-layouts  0.6 us

profile of v4, /device:TPU:25, one launch (start us, length us, event | category | flops | bytes accessed | tf_op | source)
XLA Modules:
  0.0 24.8 jit_solution(10313574026735335332)
XLA Ops:
  0.6 0.0 copy-start
  0.6 21.8 %pairformer_close.1 = (f32[512,128]{1,0:T(8,128)}, f32[4,384]{1,0:T(4,128)}) custom-call(f32[64,8,128]{2,1,0:T(8,128)} %refs_0_.1, f32[4,384]{1,0:T(4,128)} %refs_1_.1, s32[8,64]{1,0:T(8,128)} %bitcast.8, s32[4]{0:T(128)} %refs_3_.1, f32[128,512]{1,0:T(8,128)} %refs_4_.1, f32[128,512]{1,0:T(8,128)} %refs_5_.1, f32[512,128]{1,0:T(8,128)} %refs_6_.1, ...), custom_call_target="tpu_custom_call" | custom-call | tf_op jit(solution)/shard_map/pairformer_close/pallas_call | solution.py:279
  22.5 0.0 copy-done
  22.5 0.0 copy-start.1
  22.5 1.7 %bitcast_add_fusion = f32[64,8,128]{2,1,0:T(8,128)} fusion(f32[64,8,128]{2,1,0:T(8,128)S(1)} %copy-done, f32[512,128]{1,0:T(8,128)} %get-tuple-element.4), kind=kLoop, calls=%fused_computation | loop fusion | flops 65536 | bytes 786432 | tf_op jit(solution)/shard_map/add | solution.py:302
  24.2 0.0 copy-done.1
  24.2 0.6 %copy.18 = f32[4,384]{1,0:T(4,128)} copy(f32[4,384]{1,0:T(4,128)S(1)} %copy-done.1) | data formatting | bytes 12288
Async XLA Ops:
  0.6 21.9 %copy-start = (f32[64,8,128]{2,1,0:T(8,128)S(1)}, f32[64,8,128]{2,1,0:T(8,128)}, u32[]{:S(2)}) copy-start(f32[64,8,128]{2,1,0:T(8,128)} %refs_0_.1) | copy-start | bytes 786436
  22.5 1.7 %copy-start.1 = (f32[4,384]{1,0:T(4,128)S(1)}, f32[4,384]{1,0:T(4,128)}, u32[]{:S(2)}) copy-start(f32[4,384]{1,0:T(4,128)} %get-tuple-element.9) | copy-start | bytes 18436

commit v5 on v4

--- a/solution.py
+++ b/solution.py
@@ -50,8 +50,8 @@
     (pair_h, single_h, target_h, pad_s, gate_h, up_h, wout_h, wbias_h, wq_h, wk_h, wv_h, wg_h, wo_h, wdist_h, bdist_h,
      pair_o, single_o,
      pair_v, single_v, target_v, gate_v, up_v, wout_v, wbias_v, wq_v, wk_v, wv_v, wg_v, wo_v, wdist_v, bdist_v,
-     ext, gath, tokens, mid_v, proj_v, flip_v, sbuf, rbuf, bsend, brecv,
-     in_sem, g_send, g_recv, b_send, b_recv, p_send, p_recv) = refs
+     ext, gath, tokens, mid_v, proj_v, flip_v, sbuf, rbuf, tsend, trecv, bsend, brecv,
+     in_sem, g_send, g_recv, b_send, b_recv, p_send, p_recv, t_send, t_recv) = refs
     rows, cols, width = pair_v.shape
     tok, single_width = single_v.shape
     bins = wdist_v.shape[0]
@@ -124,7 +124,15 @@
     bin_rows = target_v[...].astype(F32)
     eye = (iota((rows, rows), 0) == iota((rows, rows), 1)).astype(BF16)
     filled = jnp.concatenate([bin_rows, jnp.zeros((128 - cols, rows), F32)], axis=0).astype(BF16)
-    sbuf[:, packed:, :] = mm(eye, filled, NT).reshape(group, cols, 128)
+    tsend[...] = mm(eye, filled, NT).reshape(group, cols, 128)
+
+    def send_bins(k, carry):
+        @pl.when(jnp.logical_not(is_self(k)))
+        def _():
+            pltpu.make_async_remote_copy(tsend.at[k], trecv.at[p_slot], t_send, t_recv, device_id=(p_row, group * r + k), device_id_type=MESH).start()
+        return carry
+
+    lax.fori_loop(0, group, send_bins, 0)
 
     def drain(ref, sem):
         pltpu.make_async_copy(ref, ref, sem).wait()
@@ -158,7 +166,7 @@
         halves = mid.reshape(tiles, 2, packed, width)
         both = jnp.concatenate([halves[:, 0].reshape(tiles * packed, width), halves[:, 1].reshape(tiles * packed, width)], axis=1)
         k0 = first // cols
-        sbuf[k0:k0 + tiles, :packed, :] = dot3(both, wide_w, NT).reshape(tiles, packed, 2 * bins)
+        sbuf[k0:k0 + tiles] = dot3(both, wide_w, NT).reshape(tiles, packed, 2 * bins)
         lax.fori_loop(k0, k0 + tiles, send_proj, 0)
         dests = part // tok
         norm_mid = layer_norm(mid).reshape(dests, tok, cols, width)
@@ -179,6 +187,7 @@
     @pl.when(p_row == r)
     def _():
         rbuf[p_slot] = sbuf[p_slot]
+        trecv[p_slot] = tsend[p_slot]
 
     for load in loads[8:]:
         load.wait()
@@ -218,10 +227,12 @@
 
     @pl.when(p_row == r)
     def _():
+        drain(trecv.at[pl.ds(0, group - 1)], t_recv)
         drain(rbuf.at[pl.ds(0, group - 1)], p_recv)
 
     @pl.when(p_row != r)
     def _():
+        drain(trecv, t_recv)
         drain(rbuf, p_recv)
 
     half = cols // 2
@@ -231,7 +242,7 @@
     logits = proj_v[...] + flip_v[...].reshape(total, bins) + bdist_v[...]
     expo = jnp.exp(logits - jnp.max(logits, axis=-1, keepdims=True))
     probs = expo / jnp.sum(expo, axis=-1, keepdims=True)
-    theirs = jnp.broadcast_to(rbuf[:, packed:, :cols][:, None], (group, cols, cols, cols))
+    theirs = jnp.broadcast_to(trecv[:, :, :cols][:, None], (group, cols, cols, cols))
     fours = (group, cols, cols, cols)
     theirs = jnp.where(iota(fours, 3) == iota(fours, 1), theirs, 0.0).reshape(total, cols)
     theirs = mm(theirs.astype(BF16), ones)
@@ -250,10 +261,12 @@
 
     @pl.when(p_row == r)
     def _():
+        drain(trecv.at[pl.ds(0, group - 1)], t_send)
         drain(rbuf.at[pl.ds(0, group - 1)], p_send)
 
     @pl.when(p_row != r)
     def _():
+        drain(trecv, t_send)
         drain(rbuf, p_send)
 
 
@@ -288,11 +301,13 @@
             pltpu.VMEM((rows * cols, width), F32),
             pltpu.VMEM((rows * cols, bins), F32),
             pltpu.VMEM((group, cols, cols, bins), F32),
-            pltpu.VMEM((group, packed + cols, 128), F32),
-            pltpu.VMEM((group, packed + cols, 128), F32),
+            pltpu.VMEM((group, packed, 128), F32),
+            pltpu.VMEM((group, packed, 128), F32),
+            pltpu.VMEM((group, cols, 128), F32),
+            pltpu.VMEM((group, cols, 128), F32),
             pltpu.VMEM((n_col, cols, lanes), F32),
             pltpu.VMEM((n_col, cols, lanes), F32),
-            dma((len(arrays) - 1,)), dma((3,)), dma((3,)), dma, dma, dma, dma,
+            dma((len(arrays) - 1,)), dma((3,)), dma((3,)), dma, dma, dma, dma, dma, dma,
         ],
         compiler_params=pltpu.CompilerParams(
             collective_id=0, has_side_effects=True, vmem_limit_bytes=56 * 2**20

time: 25 us -> 25 us (level)
  no operation moved by 1% of the time
where the time goes in v5:
time: 25 us; the launch traced here: 24.7 us
  Pallas kernels  21.8 us (87%)
  other arithmetic  1.69 us (7%)
  between operations  0.67 us (3%)
  local copies, waits for them, and re-layouts  0.6 us (2%)
    pallas_call x1, Pallas kernels, per_device(): pl.pallas_call(functools.partial(kernel, n_row, n_col, heads), out_shape=...  21.8 us
    add x1, other arithmetic, per_device(): return (pair + pair_out.reshape(pair.shape), single_out)  1.69 us
    unnamed x5, local copies, waits for them, and re-layouts  0.6 us

profile of v5, /device:TPU:25, one launch (start us, length us, event | category | flops | bytes accessed | tf_op | source)
XLA Modules:
  0.0 24.7 jit_solution(631394449571251430)
XLA Ops:
  0.6 0.0 copy-start
  0.6 21.8 %pairformer_close.1 = (f32[512,128]{1,0:T(8,128)}, f32[4,384]{1,0:T(4,128)}) custom-call(f32[64,8,128]{2,1,0:T(8,128)} %refs_0_.1, f32[4,384]{1,0:T(4,128)} %refs_1_.1, s32[8,64]{1,0:T(8,128)} %bitcast.8, s32[4]{0:T(128)} %refs_3_.1, f32[128,512]{1,0:T(8,128)} %refs_4_.1, f32[128,512]{1,0:T(8,128)} %refs_5_.1, f32[512,128]{1,0:T(8,128)} %refs_6_.1, ...), custom_call_target="tpu_custom_call" | custom-call | tf_op jit(solution)/shard_map/pairformer_close/pallas_call | solution.py:292
  22.4 0.0 copy-done
  22.4 0.0 copy-start.1
  22.5 1.7 %bitcast_add_fusion = f32[64,8,128]{2,1,0:T(8,128)} fusion(f32[64,8,128]{2,1,0:T(8,128)S(1)} %copy-done, f32[512,128]{1,0:T(8,128)} %get-tuple-element.4), kind=kLoop, calls=%fused_computation | loop fusion | flops 65536 | bytes 786432 | tf_op jit(solution)/shard_map/add | solution.py:317
  24.1 0.0 copy-done.1
  24.1 0.6 %copy.18 = f32[4,384]{1,0:T(4,128)} copy(f32[4,384]{1,0:T(4,128)S(1)} %copy-done.1) | data formatting | bytes 12288
Async XLA Ops:
  0.6 21.8 %copy-start = (f32[64,8,128]{2,1,0:T(8,128)S(1)}, f32[64,8,128]{2,1,0:T(8,128)}, u32[]{:S(2)}) copy-start(f32[64,8,128]{2,1,0:T(8,128)} %refs_0_.1) | copy-start | bytes 786436
  22.4 1.7 %copy-start.1 = (f32[4,384]{1,0:T(4,128)S(1)}, f32[4,384]{1,0:T(4,128)}, u32[]{:S(2)}) copy-start(f32[4,384]{1,0:T(4,128)} %get-tuple-element.9) | copy-start | bytes 18436
